TPU v7x, 32 devices: a whole 2x2x4 slice. The times are simulated.
32 devices in a mesh: sect: 8 (over z, y), grp: 4 (over x, core).
Axes of the slice: x: 2, y: 2, z: 4, core: 2. Of those that a mesh axis runs over, the one named last changes fastest.
Arguments:
- volts: bfloat16 [384, 8192], P('sect', 'grp'), may hold values from -6 to 6
- pfb_window: float32 [4, 512], replicated, may hold values from -3 to 3
- chan_order: int32 [256], replicated, may hold values from 0 to 255, each once
- delays: float32 [128, 384], replicated, may hold values from -2 to 2
- antenna_map: int32 [384], replicated, may hold values from 0 to 383, each once
- pointing: int32 [320], P('sect'), may hold values from 0 to 127
Outputs:
- vis: float32 [256, 2, 384, 384], P('grp', None, 'sect')
- beam_series: float32 [320, 16], P('sect', 'grp')
Inputs may be any that keep to these rules, and one draw needn't show every extreme that they name: `chan_order`: each channel stands in exactly one slot. `antenna_map`: each delay column is named by exactly one input row.
All inputs are finite; a program needn't handle non-finite values.
Results may differ from a plain program's by a relative error of at most 0.0071.
Values may be sent and summed in bfloat16 or wider, within the bound.
A program may use at most 64 MiB of HBM per device.

v0:
```python
import math

import jax
import jax.numpy as jnp
from jax import lax
from jax.sharding import PartitionSpec as P

NCH = 256
TAPS = 4


def passed_along(x, axis, by):
    count = lax.axis_size(axis)
    pairs = [(i, i + by) for i in range(count) if 0 <= i + by < count]
    return lax.ppermute(x, axis, pairs)


def dft_matrix(chan_order, frame_len):
    samples = jnp.arange(frame_len, dtype=jnp.int32)
    product = samples[:, None] * chan_order[None, :] % frame_len
    angles = product.astype(jnp.float32) * (2.0 * math.pi / frame_len)
    scaled = 1.0 / math.sqrt(frame_len)
    return (jnp.stack([jnp.cos(angles), -jnp.sin(angles)], axis=1) * scaled).astype(jnp.bfloat16)


def steering(delays, antenna_map, pointing, channels):
    chosen = jnp.take(delays, pointing, axis=0)
    chosen = jnp.take(chosen, antenna_map, axis=1)
    turns = (channels.astype(jnp.float32) + 0.5) * (2.0 * math.pi / NCH)
    phases = chosen[None, :, :] * turns[:, None, None]
    width_scale = 1.0 / math.sqrt(delays.shape[1])
    return (jnp.stack([jnp.cos(phases), -jnp.sin(phases)], axis=1) * width_scale).astype(
        jnp.bfloat16
    )


def per_device(volts, pfb_window, chan_order, delays, antenna_map, pointing):
    frame_len = 2 * NCH
    inputs_here = volts.shape[0]
    spectra_here = volts.shape[1] // frame_len
    frames = volts.reshape(inputs_here, spectra_here, frame_len)
    previous = passed_along(frames[:, spectra_here - (TAPS - 1) :], "grp", 1)
    extended = jnp.concatenate([previous, frames], axis=1)
    filtered = jnp.zeros((inputs_here, spectra_here, frame_len), jnp.float32)
    for tap_index in range(TAPS):
        begin = TAPS - 1 - tap_index
        filtered = (
            filtered
            + pfb_window[tap_index][None, None, :] * extended[:, begin : begin + spectra_here]
        )
    filtered = filtered.astype(jnp.bfloat16)
    dft_table = dft_matrix(chan_order, frame_len)
    spectra = jnp.einsum(
        "isn,npk->kpis", filtered, dft_table, preferred_element_type=jnp.float32
    ).astype(jnp.bfloat16)
    turned = lax.all_to_all(spectra, "grp", split_axis=0, concat_axis=3, tiled=True)
    slots_here = turned.shape[0]
    spectra_all = turned.shape[3]
    channels = lax.dynamic_slice_in_dim(chan_order, lax.axis_index("grp") * slots_here, slots_here)
    weights = steering(delays, antenna_map, pointing, channels)
    swapped = jnp.stack([turned[:, 1], -turned[:, 0]], axis=1)
    local_both = jnp.stack([turned, swapped], axis=1)
    gram_scale = 1.0 / spectra_all
    incoming = lax.all_gather(turned, "sect", axis=2, tiled=True)
    block = (
        jnp.einsum("cqpit,cpjt->cqij", local_both, incoming, preferred_element_type=jnp.float32)
        * gram_scale
    )
    mixed = jnp.einsum("cqbj,cpjt->cqpbt", weights, incoming, preferred_element_type=jnp.float32)
    beam_new = jnp.stack([mixed[:, 0, 0] - mixed[:, 1, 1], mixed[:, 0, 1] + mixed[:, 1, 0]], axis=1)
    beam_power = beam_new[:, 0] * beam_new[:, 0] + beam_new[:, 1] * beam_new[:, 1]
    partial_power = jnp.sum(beam_power, axis=0)
    beam_series = lax.psum_scatter(partial_power, "grp", scatter_dimension=1, tiled=True) * (
        1.0 / math.sqrt(NCH)
    )
    return (block, beam_series)


def solution(mesh):
    return jax.shard_map(
        per_device,
        mesh=mesh,
        in_specs=(P("sect", "grp"), P(), P(), P(), P(), P("sect")),
        out_specs=(P("grp", None, "sect", None), P("sect", "grp")),
        check_vma=False,
    )
```

profile of v0, /device:TPU:0, one launch (start us, length us, event | category | flops | bytes accessed | tf_op | source)
XLA Modules:
  0.0 129.1 jit_solution(5194566170106469470)
XLA Ops:
  7.2 0.0 copy-start
  7.2 0.0 all-gather.2.cloned.1.call-start
  7.2 1.0 copy.42
  8.2 2.4 %collective-permute-start = (bf16[48,3,512]{2,0,1:T(8,128)(2,1)S(1)}, bf16[48,3,512]{2,0,1:T(8,128)(2,1)S(1)}, u32[]{:S(2)}, u32[]{:S(2)}) collective-permute-start(bf16[48,3,512]{2,0,1:T(8,128)(2,1)S(1)} %slice.60), channel_id=1, source_target_pairs={{0,1},{1,2},{2,3},{4,5},{5,6},{6,7},{8,9},{9,10},{10,11},{12,13},{... | collective-permute-start | bytes 442376 | tf_op jit(solution)/shard_map/ppermute | solution.py:15
  10.6 2.8 %fusion.27 = (f32[512,1,256]{2,0,1:T(8,128)S(1)}, f32[512,1,256]{2,0,1:T(8,128)S(1)}) fusion(s32[256]{0:T(256)} %param.8), kind=kLoop, calls=%fused_computation.40 | loop fusion | flops 1966080 | bytes 1049600 | tf_op jit(solution)/shard_map/cos | solution.py:23
  13.4 0.9 fusion.43
  14.2 0.0 collective-permute-done
  14.2 0.0 copy-start.8
  14.3 0.0 copy-start.6
  14.3 0.9 constant_dynamic-update-slice_fusion
  15.2 1.2 fusion.9
  16.5 0.0 copy-start.9
  16.5 0.0 copy-start.7
  16.5 0.3 copy.19
  16.8 0.8 reshape.177
  17.6 9.8 %all_to_all.18 = bf16[4,2,12288]{2,1,0:T(2,128)(2,1)S(1)} all-to-all(bf16[4,2,12288]{2,1,0:T(2,128)(2,1)S(1)} %reshape.177), channel_id=1, replica_groups=mesh['sect'=8,'grp'=4] {'grp'}, dimensions={0} | all-to-all | bytes 393216 | tf_op jit(solution)/shard_map/all_to_all | solution.py:56
  27.4 0.5 reshape.178
  28.0 0.2 copy.20
  28.1 0.0 copy-start.2
  28.2 1.7 %copy.21 = bf16[64,2,48,16]{0,3,1,2:T(8,128)(2,1)} copy(bf16[64,2,48,16]{2,3,1,0:T(8,128)(2,1)S(1)} %bitcast.54) | data formatting | bytes 393216 | tf_op jit(solution)/shard_map/all_to_all | solution.py:56
  29.8 0.0 all-gather.2.cloned.1.call-update
  29.9 0.0 copy-done.8
  29.9 0.0 copy-done.6
  29.9 0.0 copy-done
  29.9 0.6 gather_fusion
  30.6 0.1 broadcast_select_fusion
  30.6 0.1 copy.23
  30.8 1.1 gather_fusion.1
  31.9 0.1 select_bitcast_fusion
  32.0 0.1 copy.24
  32.1 0.0 copy-done.9
  32.1 0.6 dynamic-slice
  33.4 0.0 copy-done.7
  33.4 0.1 add_multiply_fusion
  33.5 16.1 %multiply_cosine_fusion = (f32[64,1,40,384]{3,2,1,0:T(8,128)}, f32[64,1,40,384]{3,2,1,0:T(8,128)}) fusion(f32[64]{0:T(128)S(1)} %add_multiply_fusion, f32[40,384]{1,0:T(8,128)S(1)} %copy.24), kind=kLoop, calls=%fused_computation.6 | loop fusion | flops 1966080 | bytes 7926016 | tf_op jit(solution)/shard_map/cos | solution.py:32
  49.6 0.0 copy-done.2
  49.6 0.1 fusion.42
  49.7 0.9 maximum_bitcast_fusion
  50.6 40.1 %all-gather.2.cloned.1.call-done = bf16[64,2,384,16]{0,3,1,2:T(8,128)(2,1)} async-done(((bf16[64,2,48,16]{0,3,1,2:T(8,128)(2,1)}), bf16[64,2,384,16]{0,3,1,2:T(8,128)(2,1)}) %all-gather.2.cloned.1.call-update) | async-done | bytes 1572880 | tf_op jit(solution)/shard_map/all_gather | solution.py:64
  90.7 7.0 %copy.27 = bf16[64,2,384,16,1]{2,3,1,4,0:T(8,128)(2,1)} copy(bf16[64,2,384,16,1]{0,3,1,2,4:T(8,128)(2,1)} %bitcast.52) | data formatting | bytes 3145728 | tf_op jit(solution)/shard_map/all_gather | solution.py:64
  97.7 0.0 copy-done.1
  97.7 5.3 %copy.29 = bf16[64,2,384,16,1]{2,3,4,1,0:T(8,128)(2,1)} copy(bf16[64,2,384,16,1]{0,3,1,2,4:T(8,128)(2,1)S(1)} %bitcast.53) | data formatting | bytes 3145728 | tf_op jit(solution)/shard_map/all_gather | solution.py:64
  103.0 7.5 %fusion.6 = f32[64,2,2,40,16]{3,4,1,2,0:T(8,128)S(1)} fusion(bf16[64,2,384,16,1]{2,3,4,1,0:T(8,128)(2,1)} %copy.29, f32[64,1,40,384]{3,2,1,0:T(8,128)} %get-tuple-element.5, f32[64,1,40,384]{3,2,1,0:T(8,128)} %get-tuple-element.4), kind=kOutput, calls=%fused_computation.11 | convolution fusion | flops 131727360 | bytes 10092544 | tf_op jit(solution)/shard_map/cqbj,cpjt->cqpbt/dot_general | solution.py:69
  110.5 0.1 fusion.21
  110.6 5.8 %all-reduce = f32[40,16]{0,1:T(8,128)S(1)} all-reduce(f32[40,16]{0,1:T(8,128)S(1)} %fusion.21), channel_id=2, replica_groups=mesh['sect'=8,'grp'=4] {'grp'}, use_global_device_ids=true, to_apply=%region_1.2.clone | all-reduce | flops 640 | bytes 5120
  116.5 0.6 dynamic-slice_multiply_fusion
  117.1 0.0 copy-done.4
  117.1 5.2 %bitcast_multiply_fusion = f32[64,2,48,384]{3,2,1,0:T(8,128)} fusion(bf16[64,2,384,16,1]{2,3,1,4,0:T(8,128)(2,1)S(1)} %copy-done.4, bf16[64,1,2,48,16]{3,4,2,1,0:T(8,128)(2,1)S(1)} %copy-done.5, bf16[64,1,2,48,16]{3,4,2,1,0:T(8,128)(2,1)S(1)} %bitcast.56), kind=kOutput, calls=%fused_computation.2 | convolution fusion | flops 153550848 | bytes 11403264 | tf_op jit(solution)/shard_map/cqpit,cpjt->cqij/dot_general | solution.py:66
  (13 shorter events, 0.1 us)
Async XLA Ops:
  7.2 22.7 %copy-start = (f32[128,384]{1,0:T(8,128)S(1)}, f32[128,384]{1,0:T(8,128)}, u32[]{:S(2)}) copy-start(f32[128,384]{1,0:T(8,128)} %param.9) | copy-start | bytes 589828
  7.2 83.5 %all-gather.2.cloned.1.call-start = ((), (), s32[]{:S(2)}) async-start(), calls=%async_computation.1 | async-start | bytes 3538944 | tf_op jit(solution)/shard_map/all_gather | solution.py:64
  8.2 6.0 %collective-permute-start = (bf16[48,3,512]{2,0,1:T(8,128)(2,1)S(1)}, bf16[48,3,512]{2,0,1:T(8,128)(2,1)S(1)}, u32[]{:S(2)}, u32[]{:S(2)}) collective-permute-start(bf16[48,3,512]{2,0,1:T(8,128)(2,1)S(1)} %slice.60), channel_id=1, source_target_pairs={{0,1},{1,2},{2,3},{4,5},{5,6},{6,7},{8,9},{9,10},{10,11},{12,13},{... | collective-permute-start | bytes 442376 | tf_op jit(solution)/shard_map/ppermute | solution.py:15
  14.2 15.6 %copy-start.8 = (s32[40]{0:T(128)S(1)}, s32[40]{0:T(128)}, u32[]{:S(2)}) copy-start(s32[40]{0:T(128)} %param.11) | copy-start | bytes 484
  14.3 15.6 %copy-start.6 = (s32[384]{0:T(512)S(1)}, s32[384]{0:T(512)}, u32[]{:S(2)}) copy-start(s32[384]{0:T(512)} %param.10) | copy-start | bytes 4612
  16.5 15.7 %copy-start.9 = (u32[32]{0:T(128)S(1)}, u32[32]{0:T(128)}, u32[]{:S(2)}) copy-start(u32[32]{0:T(128)} %constant.70) | copy-start | bytes 388
  16.5 16.9 %copy-start.7 = (s32[256]{0:T(256)S(1)}, s32[256]{0:T(256)}, u32[]{:S(2)}) copy-start(s32[256]{0:T(256)} %param.8) | copy-start | bytes 3076
  28.1 21.4 %copy-start.2 = (bf16[4,64,2,48,4]{3,4,0,2,1:T(4,128)(2,1)}, bf16[4,64,2,48,4]{3,4,0,2,1:T(4,128)(2,1)S(1)}, u32[]{:S(2)}) copy-start(bf16[4,64,2,48,4]{3,4,0,2,1:T(4,128)(2,1)S(1)} %copy.20) | copy-start | bytes 589828
  90.7 7.0 %copy-start.1 = (bf16[64,2,384,16]{0,3,1,2:T(8,128)(2,1)S(1)}, bf16[64,2,384,16]{0,3,1,2:T(8,128)(2,1)}, u32[]{:S(2)}) copy-start(bf16[64,2,384,16]{0,3,1,2:T(8,128)(2,1)} %all-gather.2.cloned.1.call-done) | copy-start | bytes 4718596
  103.0 14.1 %copy-start.3 = (bf16[4,64,2,48,4]{3,4,0,2,1:T(4,128)(2,1)S(1)}, bf16[4,64,2,48,4]{3,4,0,2,1:T(4,128)(2,1)}, u32[]{:S(2)}) copy-start(bf16[4,64,2,48,4]{3,4,0,2,1:T(4,128)(2,1)} %copy-done.2) | copy-start | bytes 589828
  103.0 14.1 %copy-start.4 = (bf16[64,2,384,16,1]{2,3,1,4,0:T(8,128)(2,1)S(1)}, bf16[64,2,384,16,1]{2,3,1,4,0:T(8,128)(2,1)}, u32[]{:S(2)}) copy-start(bf16[64,2,384,16,1]{2,3,1,4,0:T(8,128)(2,1)} %copy.27) | copy-start | bytes 4718596
  103.0 14.1 %copy-start.5 = (bf16[64,1,2,48,16]{3,4,2,1,0:T(8,128)(2,1)S(1)}, bf16[64,1,2,48,16]{3,4,2,1,0:T(8,128)(2,1)}, u32[]{:S(2)}) copy-start(bf16[64,1,2,48,16]{3,4,2,1,0:T(8,128)(2,1)} %maximum_bitcast_fusion) | copy-start | bytes 589828
Sparse Core Ops, SparseCore 0:
  30.0 60.6 all-gather.1
where the time goes:
time: 129 us
  waiting for transfers between devices  40.1 us (31%)
  local copies, waits for them, and re-layouts  21.2 us (16%)
  other arithmetic  20.9 us (16%)
  blocking collectives  15.6 us (12%)
  between operations  14.9 us (12%)
  matrix products  13.9 us (11%)
  starting transfers between devices  2.4 us (2%)
    all_gather x1, waiting for transfers between devices, per_device(): incoming = lax.all_gather(turned, 'sect', axis=2, tiled=True)  40.1 us
    cos x1, other arithmetic, steering(): jnp.cos(phases)  16.1 us
    all_gather x2, local copies, waits for them, and re-layouts, per_device(): incoming = lax.all_gather(turned, 'sect', axis=2, tiled=True)  12.3 us
    all_to_all x1, blocking collectives, per_device(): lax.all_to_all(spectra, 'grp', split_axis=0, concat_axis=3, tiled=True)  9.8 us
    dot_general x1, matrix products, per_device(): jnp.einsum('cqbj,cpjt->cqpbt', weights, incoming, preferred_element_type=...  7.45 us
    unnamed x1, blocking collectives  5.84 us
    dot_general x1, matrix products, per_device(): jnp.einsum('cqpit,cpjt->cqij', local_both, incoming, preferred_element_ty...  5.18 us
    cos x1, other arithmetic, dft_matrix(): jnp.cos(angles)  2.75 us
  transfers between devices with their start and end apart: 2, of which 1 were waited for; matrix products, arithmetic and copies ran while one was open for 18% of the time, Pallas kernels for 0%

commit v1 on v0

v1 whole, which is shorter than its diff:
```python
import functools
import math

import jax
import jax.numpy as jnp
import numpy as np
from jax import lax
from jax.experimental import pallas as pl
from jax.experimental.pallas import tpu as pltpu
from jax.sharding import PartitionSpec as P

NCH = 256
TAPS = 4
FRAME = 2 * NCH
BLOCK = 512
MESH = pl.DeviceIdType.MESH


def round_up(n, m):
    return -(-n // m) * m


def cos_fit(degree):
    nodes = 0.125 + 0.125 * np.cos(np.pi * (np.arange(64) + 0.5) / 64)
    fit = np.polynomial.chebyshev.Chebyshev.fit(
        nodes, np.cos(2 * np.pi * np.sqrt(nodes)), degree, domain=[0.0, 0.25]
    )
    return [float(c) for c in fit.convert(kind=np.polynomial.Polynomial).coef]


COS = cos_fit(6)


def cos_turns(u, scale):
    r = u - jnp.round(u)
    y = r * r
    total = jnp.full_like(y, COS[-1] * scale)
    for c in COS[-2::-1]:
        total = total * y + c * scale
    return total


def dot(a, b, dims=((1,), (0,))):
    return lax.dot_general(a, b, (dims, ((), ())), preferred_element_type=jnp.float32)


def pieces(x):
    hi = x.astype(jnp.bfloat16)
    rest = x - hi.astype(jnp.float32)
    mid = rest.astype(jnp.bfloat16)
    low = (rest - mid.astype(jnp.float32)).astype(jnp.bfloat16)
    return hi, mid, low


def one_hot(rows, cols):
    return jnp.where(rows == cols, 1.0, 0.0).astype(jnp.bfloat16)


def iota(shape, dim):
    return lax.broadcasted_iota(jnp.int32, shape, dim)


def gather_kernel(
    dims,
    volts, pfb, chan_row, chan, delays, amap, pointing,
    gathered, series,
    halo, table, place, merge, turns, weights, sent, got, spec, power,
    halo_sem, turn_send, turn_recv, far_send, far_recv, near_send, near_recv,
    beam_send, beam_recv, out_sem,
):
    ns, ng, slots, here, th, inputs, beams = dims
    total = th * ng
    lanes_g = round_up(2 * slots, 128)
    chunk = sent.shape[2]
    blocks = NCH * 2 * th // BLOCK
    per_block = BLOCK // (2 * total)
    width = max(128, 2 * total)
    per_tile = width // (2 * total)
    tiles = BLOCK // width
    brows = turns.shape[0]
    inner = 2 if ns % 2 == 0 else 1
    outer = ns // inner

    sect = lax.axis_index("sect")
    grp = lax.axis_index("grp")
    row = sect // inner
    col = sect % inner

    def grp_peer(d):
        return lax.rem(grp + d, ng)

    def far_peer(d):
        return lax.rem(row + d, outer)

    barrier = pltpu.get_barrier_semaphore()
    for d in range(1, ng):
        pl.semaphore_signal(barrier, inc=1, device_id=(sect, grp_peer(d)), device_id_type=MESH)
    for d in range(1, outer):
        pl.semaphore_signal(
            barrier, inc=1, device_id=(far_peer(d) * inner + col, grp), device_id_type=MESH
        )
    if inner == 2:
        pl.semaphore_signal(
            barrier, inc=1, device_id=(row * inner + 1 - col, grp), device_id_type=MESH
        )

    def rows_of(s):
        return pl.ds(pl.multiple_of(s * here, 16), here)

    pl.semaphore_wait(barrier, (ng - 1) + (outer - 1) + (inner - 1))

    keep = TAPS - 1
    halo_copy = pltpu.make_async_remote_copy(
        src_ref=volts.at[:, (th - keep) * FRAME :],
        dst_ref=halo,
        send_sem=halo_sem.at[0],
        recv_sem=halo_sem.at[1],
        device_id=(sect, lax.rem(grp + 1, ng)),
        device_id_type=MESH,
    )

    @pl.when(grp < ng - 1)
    def _():
        halo_copy.start()

    columns = ng * lanes_g
    c = iota((NCH, columns), 1)
    slot = jnp.where(
        c % lanes_g < 2 * slots, (c // lanes_g) * slots + (c % lanes_g) // 2, -1
    )
    expand = one_hot(iota((NCH, columns), 0), slot)
    chan8 = jnp.broadcast_to(chan_row[...].astype(jnp.float32), (8, NCH)).astype(jnp.bfloat16)
    chan_cols = dot(chan8, expand)[0:1, :]
    step = 128
    quarter = (iota((1, columns), 1) % 2).astype(jnp.float32) * 0.25
    for begin in range(0, FRAME, step):
        n = (iota((step, columns), 0) + begin).astype(jnp.float32)
        angle = n * chan_cols * (1.0 / FRAME) + quarter
        table[begin : begin + step, :] = cos_turns(angle, 1.0 / math.sqrt(FRAME)).astype(
            jnp.bfloat16
        )

    k = iota((th * lanes_g, chunk), 0)
    c = iota((th * lanes_g, chunk), 1)
    place[...] = one_hot(k, (c % th) * lanes_g + c // th)

    need = per_block * 2 * th
    span = need if need % 128 == 0 else chunk

    def merge_matrix(offset):
        k = iota((ng * span, BLOCK), 0)
        c = iota((ng * span, BLOCK), 1)
        return one_hot(k, ((c % total) // th) * span + (c // total) * th + c % th + offset)

    if span == need:
        merge[...] = merge_matrix(0)

    @pl.when(grp == 0)
    def _():
        halo[...] = jnp.zeros_like(halo)

    @pl.when(grp > 0)
    def _():
        halo_copy.wait_recv()

    frames = [halo[:, i * FRAME : (i + 1) * FRAME].astype(jnp.float32) for i in range(keep)]
    frames += [volts[:, i * FRAME : (i + 1) * FRAME].astype(jnp.float32) for i in range(th)]
    filtered = []
    for t in range(th):
        value = pfb[0:1, :] * frames[t + keep]
        for tap in range(1, TAPS):
            value = value + pfb[tap : tap + 1, :] * frames[t + keep - tap]
        filtered.append(value.astype(jnp.bfloat16))
    filtered = jnp.concatenate(filtered, axis=0)
    made = dot(filtered, table[...]).astype(jnp.bfloat16)
    for g in range(ng):
        flat = jnp.concatenate(
            [
                made[t * here : (t + 1) * here, g * lanes_g : (g + 1) * lanes_g]
                for t in range(th)
            ],
            axis=1,
        )
        sent[g] = dot(flat, place[...]).astype(jnp.bfloat16)

    turn_copies = []
    for d in range(1, ng):
        peer = grp_peer(d)
        copy = pltpu.make_async_remote_copy(
            src_ref=sent.at[peer],
            dst_ref=got.at[grp],
            send_sem=turn_send.at[d],
            recv_sem=turn_recv.at[d],
            device_id=(sect, peer),
            device_id_type=MESH,
        )
        copy.start()
        turn_copies.append(copy)
    got[grp] = sent[grp]

    b = beams
    eye = iota((b, b), 0) == iota((b, b), 1)
    spread = jnp.broadcast_to(pointing[...].astype(jnp.float32), (b, b))
    point_col = jnp.sum(jnp.where(eye, spread, 0.0), axis=1, keepdims=True).astype(jnp.int32)
    points = delays.shape[0]
    pick = one_hot(iota((b, points), 1), jnp.broadcast_to(point_col, (b, points)))
    hi, mid, low = pieces(delays[...])
    chosen = (dot(pick, hi) + dot(pick, mid)) + dot(pick, low)
    order = one_hot(
        iota((inputs, inputs), 0), jnp.broadcast_to(amap[...], (inputs, inputs))
    )
    hi, mid, low = pieces(chosen)
    chosen = (dot(hi, order) + dot(mid, order)) + dot(low, order)
    turns[...] = jnp.zeros_like(turns)
    turns[0:b, :] = chosen * (1.0 / NCH)

    for copy in turn_copies:
        copy.wait_recv()

    mine = rows_of(sect)
    for q in range(blocks):
        begin = q * need if span == need else 0
        flat = jnp.concatenate(
            [got[g, :, begin : begin + span] for g in range(ng)], axis=1
        )
        matrix = merge[...] if span == need else merge_matrix(q * need)
        spec[q, mine, :] = dot(flat, matrix).astype(jnp.bfloat16)

    def far_copy(q, d):
        return pltpu.make_async_remote_copy(
            src_ref=spec.at[q, mine, :],
            dst_ref=spec.at[q, mine, :],
            send_sem=far_send.at[q, d],
            recv_sem=far_recv.at[q, d],
            device_id=(far_peer(d) * inner + col, grp),
            device_id_type=MESH,
        )

    def near_copy(q, d):
        begun = rows_of(lax.rem(row - d + outer, outer) * inner + col)
        return pltpu.make_async_remote_copy(
            src_ref=spec.at[q, begun, :],
            dst_ref=spec.at[q, begun, :],
            send_sem=near_send.at[q, d],
            recv_sem=near_recv.at[q, d],
            device_id=(row * inner + 1 - col, grp),
            device_id_type=MESH,
        )

    for q in range(blocks):
        for d in range(1, outer):
            far_copy(q, d).start()
        if inner == 2:
            near_copy(q, 0).start()

    scale = 1.0 / math.sqrt(inputs)

    def weigh(tile):
        for k in range(per_tile):
            channel = chan[grp * slots + tile * per_tile + k].astype(jnp.float32) + 0.5
            for part in range(2):
                at = (k * 2 + part) * brows
                weights[tile, at : at + brows, :] = cos_turns(
                    turns[...] * channel + 0.25 * part, scale
                ).astype(jnp.bfloat16)

    for q in range(blocks):
        pl.loop(q * tiles, (q + 1) * tiles)(weigh)
        for d in range(1, outer):
            far_copy(q, d).wait_recv()
            if inner == 2:
                near_copy(q, d).start()

    lane = iota((brows, width), 1)
    slot_in = lane // (2 * total)
    first = (lane // total) % 2 == 0
    out_copies = []
    power[ng] = jnp.zeros_like(power[ng])
    acc = jnp.zeros((brows, width), jnp.float32)
    for q in range(blocks):
        if inner == 2:
            for d in range(outer):
                near_copy(q, d).wait_recv()
        copy = pltpu.make_async_copy(spec.at[q], gathered.at[q], out_sem.at[q])
        copy.start()
        out_copies.append(copy)
        for i in range(tiles):
            data = spec[q, :, i * width : (i + 1) * width]
            mixed = dot(weights[q * tiles + i], data)
            both = []
            for part in range(2):
                picked = jnp.zeros((brows, width), jnp.float32)
                for k in range(per_tile):
                    at = (k * 2 + part) * brows
                    picked = jnp.where(slot_in == k, mixed[at : at + brows, :], picked)
                both.append(picked)
            forward = pltpu.roll(both[1], total, 1)
            backward = pltpu.roll(both[1], width - total, 1)
            beam = both[0] + jnp.where(first, -backward, forward)
            acc = acc + beam * beam
    shift = width // 2
    while shift >= total:
        acc = acc + pltpu.roll(acc, shift, 1)
        shift //= 2
    power[ng] = acc[:, : power.shape[2]]

    beam_copies = []
    for d in range(1, ng):
        copy = pltpu.make_async_remote_copy(
            src_ref=power.at[ng],
            dst_ref=power.at[d],
            send_sem=beam_send.at[d],
            recv_sem=beam_recv.at[d],
            device_id=(sect, grp_peer(d)),
            device_id_type=MESH,
        )
        copy.start()
        beam_copies.append(copy)
    for q in range(blocks):
        for d in range(1, outer):
            far_copy(q, d).wait_send()
        if inner == 2:
            for d in range(outer):
                near_copy(q, d).wait_send()
    for copy in turn_copies:
        copy.wait_send()

    @pl.when(grp < ng - 1)
    def _():
        halo_copy.wait_send()

    for copy in out_copies:
        copy.wait()
    summed = power[ng]
    for d, copy in enumerate(beam_copies):
        copy.wait_recv()
        summed = summed + power[d + 1]
    lanes = summed.shape[1]
    turned = pltpu.roll(summed, lax.rem(lanes - grp * th, lanes), 1)
    series[...] = turned[:beams, :th] * (1.0 / math.sqrt(NCH))
    for copy in beam_copies:
        copy.wait_send()


def vis_kernel(here, total, per_tile, tiles, spec, vis):
    width = spec.shape[2] // tiles
    mine = pl.ds(pl.multiple_of(lax.axis_index("sect") * here, 16), here)
    lane = iota((here, width), 1)
    slot_in = lane // (2 * total)
    first = (lane // total) % 2 == 0
    for i in range(tiles):
        cols = slice(i * width, (i + 1) * width)
        local = spec[0, mine, cols].astype(jnp.float32)
        forward = pltpu.roll(local, total, 1)
        backward = pltpu.roll(local, width - total, 1)
        swapped = jnp.where(first, backward, -forward)
        left = []
        for k in range(per_tile):
            for part in (local, swapped):
                left.append(jnp.where(slot_in == k, part, 0.0).astype(jnp.bfloat16))
        block = dot(jnp.concatenate(left, axis=0), spec[0, :, cols], ((1,), (1,)))
        block = block * (1.0 / total)
        for k in range(per_tile):
            for part in range(2):
                at = (k * 2 + part) * here
                vis[i * per_tile + k, part] = block[at : at + here, :]


def per_device(ns, ng, volts, pfb_window, chan_order, delays, antenna_map, pointing):
    here = volts.shape[0]
    th = volts.shape[1] // FRAME
    inputs = delays.shape[1]
    beams = pointing.shape[0]
    slots = NCH // ng
    total = th * ng
    brows = round_up(beams, 16)
    lanes_g = round_up(2 * slots, 128)
    chunk = round_up(2 * slots * th, 128)
    blocks = NCH * 2 * th // BLOCK
    width = max(128, 2 * total)
    per_tile = width // (2 * total)
    tiles = BLOCK // width
    need = BLOCK // (2 * total) * 2 * th
    span = need if need % 128 == 0 else chunk
    outer = ns // 2 if ns % 2 == 0 else ns
    bf16, f32 = jnp.bfloat16, jnp.float32
    vmem = pl.BlockSpec(memory_space=pltpu.VMEM)
    dims = (ns, ng, slots, here, th, inputs, beams)
    dma = pltpu.SemaphoreType.DMA
    gathered, series = pl.pallas_call(
        functools.partial(gather_kernel, dims),
        out_shape=(
            jax.ShapeDtypeStruct((blocks, inputs, BLOCK), bf16),
            jax.ShapeDtypeStruct((beams, th), f32),
        ),
        in_specs=[vmem, vmem, vmem, pl.BlockSpec(memory_space=pltpu.SMEM), vmem, vmem, vmem],
        out_specs=(pl.BlockSpec(memory_space=pl.ANY), vmem),
        scratch_shapes=[
            pltpu.VMEM((here, (TAPS - 1) * FRAME), bf16),
            pltpu.VMEM((FRAME, ng * lanes_g), bf16),
            pltpu.VMEM((th * lanes_g, chunk), bf16),
            pltpu.VMEM((ng * span, BLOCK), bf16),
            pltpu.VMEM((brows, inputs), f32),
            pltpu.VMEM((blocks * tiles, per_tile * 2 * brows, inputs), bf16),
            pltpu.VMEM((ng, here, chunk), bf16),
            pltpu.VMEM((ng, here, chunk), bf16),
            pltpu.VMEM((blocks, inputs, BLOCK), bf16),
            pltpu.VMEM((ng + 1, brows, round_up(total, 128)), f32),
            dma((2,)),
            dma((ng,)),
            dma((ng,)),
            dma((blocks, outer)),
            dma((blocks, outer)),
            dma((blocks, outer)),
            dma((blocks, outer)),
            dma((ng,)),
            dma((ng,)),
            dma((blocks,)),
        ],
        compiler_params=pltpu.CompilerParams(
            collective_id=0, has_side_effects=True, vmem_limit_bytes=48 * 1024 * 1024
        ),
    )(
        volts,
        pfb_window,
        chan_order.reshape(1, -1),
        chan_order,
        delays,
        antenna_map.reshape(1, -1),
        pointing.reshape(1, -1),
    )
    vis = pl.pallas_call(
        functools.partial(vis_kernel, here, total, per_tile, tiles),
        grid=(blocks,),
        out_shape=jax.ShapeDtypeStruct((slots, 2, here, inputs), f32),
        in_specs=[pl.BlockSpec((1, inputs, BLOCK), lambda q: (q, 0, 0))],
        out_specs=pl.BlockSpec(
            (slots // blocks, 2, here, inputs), lambda q: (q, 0, 0, 0)
        ),
        compiler_params=pltpu.CompilerParams(vmem_limit_bytes=48 * 1024 * 1024),
    )(gathered)
    return (vis, series)


def solution(mesh):
    ns, ng = mesh.shape["sect"], mesh.shape["grp"]
    return jax.shard_map(
        functools.partial(per_device, ns, ng),
        mesh=mesh,
        in_specs=(P("sect", "grp"), P(), P(), P(), P(), P("sect")),
        out_specs=(P("grp", None, "sect", None), P("sect", "grp")),
        check_vma=False,
    )
```

time: 129 us -> 50.6 us (0.39)
  Pallas kernels: 0 us -> 44.5 us
  waiting for transfers between devices: 40.1 us -> 0 us
  other arithmetic: 20.9 us -> 0 us
  local copies, waits for them, and re-layouts: 21.2 us -> 5.22 us
  blocking collectives: 15.6 us -> 0 us
  between operations: 14.9 us -> 0.64 us
  matrix products: 13.9 us -> 0 us
  starting transfers between devices: 2.4 us -> 0 us
    pallas_call x0 -> x2, Pallas kernels: none -> 44.5 us  [the longest x1 39.9 us: per_device(): pl.pallas_call(functools.partial(gather_kernel, dims), out_shape=(jax.Sha...]
    all_gather x1 -> x0, waiting for transfers between devices: 40.1 us -> none  [per_device(): incoming = lax.all_gather(turned, 'sect', axis=2, tiled=True)]
    cos x2 -> x0, other arithmetic: 18.9 us -> none  [the longest x1 16.1 us: steering(): jnp.cos(phases)]
    dot_general x3 -> x0, matrix products: 13.9 us -> none  [the longest x1 7.45 us: per_device(): jnp.einsum('cqbj,cpjt->cqpbt', weights, incoming, preferred_element_type=...]
    all_gather x2 -> x0, local copies, waits for them, and re-layouts: 12.3 us -> none  [per_device(): incoming = lax.all_gather(turned, 'sect', axis=2, tiled=True)]
    all_to_all x1 -> x0, blocking collectives: 9.8 us -> none  [per_device(): lax.all_to_all(spectra, 'grp', split_axis=0, concat_axis=3, tiled=True)]
    unnamed x1 -> x0, blocking collectives: 5.84 us -> none
    unnamed x24 -> x11, local copies, waits for them, and re-layouts: 1.98 us -> 4.53 us
  transfers between devices with their start and end apart: 2 -> 0, of which waited for: 1 -> 0; matrix products, arithmetic and copies ran while one was open for 18% -> 0% of each run, Pallas kernels for 0% -> 0%
where the time goes in v1:
time: 50.6 us; the launch traced here: 50.4 us
  Pallas kernels  44.5 us (88%)
  local copies, waits for them, and re-layouts  5.22 us (10%)
  between operations  0.64 us (1%)
    pallas_call x1, Pallas kernels, per_device(): pl.pallas_call(functools.partial(gather_kernel, dims), out_shape=(jax.Sha...  39.9 us
    pallas_call x1, Pallas kernels, per_device(): pl.pallas_call(functools.partial(vis_kernel, here, total, per_tile, tiles...  4.62 us
    unnamed x11, local copies, waits for them, and re-layouts  4.53 us

profile of v1, /device:TPU:0, one launch (start us, length us, event | category | flops | bytes accessed | tf_op | source)
XLA Modules:
  0.0 50.4 jit_solution(14417460914120453450)
XLA Ops:
  0.6 0.7 %reshape.14.amap = s32[1,384]{1,0:T(1,128)S(1)} reshape(s32[384]{0:T(512)} %param.10) | data formatting | bytes 3072 | tf_op jit(solution)/shard_map/reshape | solution.py:429
  1.3 0.0 copy-start
  1.3 0.9 %copy-done = bf16[48,2048]{1,0:T(8,128)(2,1)S(1)} copy-done((bf16[48,2048]{1,0:T(8,128)(2,1)S(1)}, bf16[48,2048]{1,0:T(8,128)(2,1)}, u32[]{:S(2)}) %copy-start) | copy-done | bytes 196632
  2.2 0.0 copy-start.1
  2.2 0.9 %copy-done.1 = f32[128,384]{1,0:T(8,128)S(1)} copy-done((f32[128,384]{1,0:T(8,128)S(1)}, f32[128,384]{1,0:T(8,128)}, u32[]{:S(2)}) %copy-start.1) | copy-done | bytes 196632
  3.2 0.0 copy-start.2
  3.2 0.7 %copy-done.2 = f32[4,512]{1,0:T(4,128)S(1)} copy-done((f32[4,512]{1,0:T(4,128)S(1)}, f32[4,512]{1,0:T(4,128)}, u32[]{:S(2)}) %copy-start.2) | copy-done | bytes 8216
  3.9 0.0 copy-start.3
  3.9 0.7 %copy-done.3 = s32[256]{0:T(256)S(1)} copy-done((s32[256]{0:T(256)S(1)}, s32[256]{0:T(256)}, u32[]{:S(2)}) %copy-start.3) | copy-done | bytes 1048
  4.5 0.0 copy-start.4
  4.5 0.7 %copy-done.4 = s32[40]{0:T(128)S(1)} copy-done((s32[40]{0:T(128)S(1)}, s32[40]{0:T(128)}, u32[]{:S(2)}) %copy-start.4) | copy-done | bytes 184
  5.2 39.9 %shard_map.77 = (bf16[4,384,512]{2,1,0:T(8,128)(2,1)S(1)}, f32[40,4]{1,0:T(8,128)S(1)}) custom-call(bf16[48,2048]{1,0:T(8,128)(2,1)S(1)} %copy-done, f32[4,512]{1,0:T(4,128)S(1)} %copy-done.2, s32[1,256]{1,0:T(1,128)S(1)} %bitcast.2, s32[256]{0:T(256)S(1)} %copy-done.3, f32[128,384]{1,0:T(8,128)S(1)} %copy-done.1, s32[1,384]{1,0:T(1,128)S(1)} %reshape.14.amap, ...), custom_call_target="tpu_custom_call" | custom-call | tf_op jit(solution)/shard_map/pallas_call | solution.py:390
  45.1 0.7 %copy.8 = f32[40,4]{0,1:T(4,128)} copy(f32[40,4]{1,0:T(8,128)S(1)} %get-tuple-element.7) | data formatting | bytes 1280
  45.8 4.6 %shard_map.78 = f32[64,2,48,384]{3,2,1,0:T(8,128)} custom-call(bf16[4,384,512]{2,1,0:T(8,128)(2,1)S(1)} %get-tuple-element.4.spec), custom_call_target="tpu_custom_call" | custom-call | tf_op jit(solution)/shard_map/pallas_call | solution.py:432
Async XLA Ops:
  1.3 0.9 %copy-start = (bf16[48,2048]{1,0:T(8,128)(2,1)S(1)}, bf16[48,2048]{1,0:T(8,128)(2,1)}, u32[]{:S(2)}) copy-start(bf16[48,2048]{1,0:T(8,128)(2,1)} %volts.1) | copy-start | bytes 589828
  2.2 0.9 %copy-start.1 = (f32[128,384]{1,0:T(8,128)S(1)}, f32[128,384]{1,0:T(8,128)}, u32[]{:S(2)}) copy-start(f32[128,384]{1,0:T(8,128)} %delays.1) | copy-start | bytes 589828
  3.2 0.7 %copy-start.2 = (f32[4,512]{1,0:T(4,128)S(1)}, f32[4,512]{1,0:T(4,128)}, u32[]{:S(2)}) copy-start(f32[4,512]{1,0:T(4,128)} %pfb.1) | copy-start | bytes 24580
  3.9 0.7 %copy-start.3 = (s32[256]{0:T(256)S(1)}, s32[256]{0:T(256)}, u32[]{:S(2)}) copy-start(s32[256]{0:T(256)} %chan.1) | copy-start | bytes 3076
  4.5 0.7 %copy-start.4 = (s32[40]{0:T(128)S(1)}, s32[40]{0:T(128)}, u32[]{:S(2)}) copy-start(s32[40]{0:T(128)} %param.11) | copy-start | bytes 484

commit v2 on v1

--- a/solution.py
+++ b/solution.py
@@ -62,11 +62,12 @@
 
 def gather_kernel(
     dims,
-    volts, pfb, chan_row, chan, delays, amap, pointing,
+    volts_in, pfb_in, chan_in, chan, delays_in, amap_in, pointing_in,
     gathered, series,
+    volts, pfb, chan_row, delays, amap, pointing, in_sem,
     halo, table, place, merge, turns, weights, sent, got, spec, power,
-    halo_sem, turn_send, turn_recv, far_send, far_recv, near_send, near_recv,
-    beam_send, beam_recv, out_sem,
+    halo_sem, turn_send, turn_recv, line_send, line_recv, near_send, near_recv,
+    extra_send, extra_recv, beam_send, beam_recv, out_sem,
 ):
     ns, ng, slots, here, th, inputs, beams = dims
     total = th * ng
@@ -89,29 +90,42 @@
     def grp_peer(d):
         return lax.rem(grp + d, ng)
 
-    def far_peer(d):
-        return lax.rem(row + d, outer)
-
     barrier = pltpu.get_barrier_semaphore()
     for d in range(1, ng):
         pl.semaphore_signal(barrier, inc=1, device_id=(sect, grp_peer(d)), device_id_type=MESH)
-    for d in range(1, outer):
-        pl.semaphore_signal(
-            barrier, inc=1, device_id=(far_peer(d) * inner + col, grp), device_id_type=MESH
-        )
+    for way in (1, -1):
+
+        @pl.when((row + way >= 0) & (row + way < outer))
+        def _(way=way):
+            pl.semaphore_signal(
+                barrier, inc=1, device_id=((row + way) * inner + col, grp), device_id_type=MESH
+            )
+
     if inner == 2:
         pl.semaphore_signal(
             barrier, inc=1, device_id=(row * inner + 1 - col, grp), device_id_type=MESH
         )
 
+    loads = []
+    operands = ((chan_in, chan_row.at[0]), (volts_in, volts), (pfb_in, pfb),
+                (delays_in, delays), (amap_in, amap.at[0]), (pointing_in, pointing.at[0]))
+    for at, (src, dst) in enumerate(operands):
+        loads.append(pltpu.make_async_copy(src, dst, in_sem.at[at]))
+        loads[-1].start()
+
     def rows_of(s):
         return pl.ds(pl.multiple_of(s * here, 16), here)
 
-    pl.semaphore_wait(barrier, (ng - 1) + (outer - 1) + (inner - 1))
+    k = iota((th * lanes_g, chunk), 0)
+    c = iota((th * lanes_g, chunk), 1)
+    place[...] = one_hot(k, (c % th) * lanes_g + c // th)
+
+    in_line = (row > 0).astype(jnp.int32) + (row < outer - 1).astype(jnp.int32)
+    pl.semaphore_wait(barrier, (ng - 1) + (inner - 1) + in_line)
 
     keep = TAPS - 1
     halo_copy = pltpu.make_async_remote_copy(
-        src_ref=volts.at[:, (th - keep) * FRAME :],
+        src_ref=volts_in.at[:, (th - keep) * FRAME :],
         dst_ref=halo,
         send_sem=halo_sem.at[0],
         recv_sem=halo_sem.at[1],
@@ -123,6 +137,7 @@
     def _():
         halo_copy.start()
 
+    loads[0].wait()
     columns = ng * lanes_g
     c = iota((NCH, columns), 1)
     slot = jnp.where(
@@ -140,10 +155,6 @@
             jnp.bfloat16
         )
 
-    k = iota((th * lanes_g, chunk), 0)
-    c = iota((th * lanes_g, chunk), 1)
-    place[...] = one_hot(k, (c % th) * lanes_g + c // th)
-
     need = per_block * 2 * th
     span = need if need % 128 == 0 else chunk
 
@@ -154,6 +165,24 @@
 
     if span == need:
         merge[...] = merge_matrix(0)
+
+    for load in loads[1:]:
+        load.wait()
+    b = beams
+    eye = iota((b, b), 0) == iota((b, b), 1)
+    spread = jnp.broadcast_to(pointing[...].astype(jnp.float32), (b, b))
+    point_col = jnp.sum(jnp.where(eye, spread, 0.0), axis=1, keepdims=True).astype(jnp.int32)
+    points = delays.shape[0]
+    pick = one_hot(iota((b, points), 1), jnp.broadcast_to(point_col, (b, points)))
+    hi, mid, low = pieces(delays[...])
+    chosen = (dot(pick, hi) + dot(pick, mid)) + dot(pick, low)
+    order = one_hot(
+        iota((inputs, inputs), 0), jnp.broadcast_to(amap[...], (inputs, inputs))
+    )
+    hi, mid, low = pieces(chosen)
+    chosen = (dot(hi, order) + dot(mid, order)) + dot(low, order)
+    turns[...] = jnp.zeros_like(turns)
+    turns[0:b, :] = chosen * (1.0 / NCH)
 
     @pl.when(grp == 0)
     def _():
@@ -183,75 +212,108 @@
         )
         sent[g] = dot(flat, place[...]).astype(jnp.bfloat16)
 
-    turn_copies = []
-    for d in range(1, ng):
+    parts = blocks if span == need else 1
+
+    def turn_copy(q, d):
         peer = grp_peer(d)
-        copy = pltpu.make_async_remote_copy(
-            src_ref=sent.at[peer],
-            dst_ref=got.at[grp],
-            send_sem=turn_send.at[d],
-            recv_sem=turn_recv.at[d],
+        lanes = pl.ds(q * span, span)
+        return pltpu.make_async_remote_copy(
+            src_ref=sent.at[peer, :, lanes],
+            dst_ref=got.at[grp, :, lanes],
+            send_sem=turn_send.at[q, d],
+            recv_sem=turn_recv.at[q, d],
             device_id=(sect, peer),
             device_id_type=MESH,
         )
-        copy.start()
-        turn_copies.append(copy)
-    got[grp] = sent[grp]
-
-    b = beams
-    eye = iota((b, b), 0) == iota((b, b), 1)
-    spread = jnp.broadcast_to(pointing[...].astype(jnp.float32), (b, b))
-    point_col = jnp.sum(jnp.where(eye, spread, 0.0), axis=1, keepdims=True).astype(jnp.int32)
-    points = delays.shape[0]
-    pick = one_hot(iota((b, points), 1), jnp.broadcast_to(point_col, (b, points)))
-    hi, mid, low = pieces(delays[...])
-    chosen = (dot(pick, hi) + dot(pick, mid)) + dot(pick, low)
-    order = one_hot(
-        iota((inputs, inputs), 0), jnp.broadcast_to(amap[...], (inputs, inputs))
-    )
-    hi, mid, low = pieces(chosen)
-    chosen = (dot(hi, order) + dot(mid, order)) + dot(low, order)
-    turns[...] = jnp.zeros_like(turns)
-    turns[0:b, :] = chosen * (1.0 / NCH)
-
-    for copy in turn_copies:
-        copy.wait_recv()
+
+    for q in range(parts):
+        for d in range(1, ng):
+            turn_copy(q, d).start()
 
     mine = rows_of(sect)
-    for q in range(blocks):
-        begin = q * need if span == need else 0
-        flat = jnp.concatenate(
-            [got[g, :, begin : begin + span] for g in range(ng)], axis=1
-        )
-        matrix = merge[...] if span == need else merge_matrix(q * need)
-        spec[q, mine, :] = dot(flat, matrix).astype(jnp.bfloat16)
-
-    def far_copy(q, d):
+
+    def begun(way, k):
+        return lax.rem(row - way * k + 2 * outer, outer)
+
+    def line_copy(way, q, k, block):
+        at = rows_of(block * inner + col)
         return pltpu.make_async_remote_copy(
-            src_ref=spec.at[q, mine, :],
-            dst_ref=spec.at[q, mine, :],
-            send_sem=far_send.at[q, d],
-            recv_sem=far_recv.at[q, d],
-            device_id=(far_peer(d) * inner + col, grp),
+            src_ref=spec.at[q, at, :],
+            dst_ref=spec.at[q, at, :],
+            send_sem=line_send.at[(1 - way) // 2, q, k],
+            recv_sem=line_recv.at[(1 - way) // 2, q, k],
+            device_id=(lax.rem(row + way + outer, outer) * inner + col, grp),
             device_id_type=MESH,
         )
 
-    def near_copy(q, d):
-        begun = rows_of(lax.rem(row - d + outer, outer) * inner + col)
+    def near_copy(q, d, mirrored):
+        at = rows_of(begun(1, d) * inner + (1 - col if mirrored else col))
         return pltpu.make_async_remote_copy(
-            src_ref=spec.at[q, begun, :],
-            dst_ref=spec.at[q, begun, :],
+            src_ref=spec.at[q, at, :],
+            dst_ref=spec.at[q, at, :],
             send_sem=near_send.at[q, d],
             recv_sem=near_recv.at[q, d],
             device_id=(row * inner + 1 - col, grp),
             device_id_type=MESH,
         )
 
+    def extra_copy(way, q, block):
+        at = rows_of(block * inner + 1 - col)
+        return pltpu.make_async_remote_copy(
+            src_ref=spec.at[q, at, :],
+            dst_ref=spec.at[q, at, :],
+            send_sem=extra_send.at[(1 - way) // 2, q],
+            recv_sem=extra_recv.at[(1 - way) // 2, q],
+            device_id=(lax.rem(row + way + outer, outer) * inner + col, grp),
+            device_id_type=MESH,
+        )
+
+    def has_next(way):
+        return row < outer - 1 if way == 1 else row > 0
+
+    def has_behind(way, k):
+        return row >= k if way == 1 else row + k < outer
+
+    spare = [q for q in range(blocks) if q >= blocks // 2] if inner == 2 and outer > 3 else []
+
+    def by_line(q, d):
+        if q not in spare:
+            return None
+        if d == outer - 1:
+            return row == 0
+        if d == 1:
+            return row == outer - 1
+        return None
+
+    def near_do(q, d, act):
+        skip = by_line(q, d)
+        if skip is None:
+            act()
+        else:
+            pl.when(jnp.logical_not(skip))(act)
+
     for q in range(blocks):
-        for d in range(1, outer):
-            far_copy(q, d).start()
+        if q < parts:
+            for d in range(1, ng):
+                turn_copy(q, d).wait_recv()
+        begin = q * need if span == need else 0
+        flat = jnp.concatenate(
+            [
+                jnp.where(grp == g, sent[g, :, begin : begin + span], got[g, :, begin : begin + span])
+                for g in range(ng)
+            ],
+            axis=1,
+        )
+        matrix = merge[...] if span == need else merge_matrix(q * need)
+        spec[q, mine, :] = dot(flat, matrix).astype(jnp.bfloat16)
+        for way in (1, -1):
+
+            @pl.when(has_next(way))
+            def _():
+                line_copy(way, q, 0, row).start()
+
         if inner == 2:
-            near_copy(q, 0).start()
+            near_copy(q, 0, False).start()
 
     scale = 1.0 / math.sqrt(inputs)
 
@@ -264,12 +326,40 @@
                     turns[...] * channel + 0.25 * part, scale
                 ).astype(jnp.bfloat16)
 
-    for q in range(blocks):
-        pl.loop(q * tiles, (q + 1) * tiles)(weigh)
-        for d in range(1, outer):
-            far_copy(q, d).wait_recv()
-            if inner == 2:
-                near_copy(q, d).start()
+    steps = max(1, (outer - 1) * blocks)
+    count = blocks * tiles
+    for k in range(1, outer):
+        for q in range(blocks):
+            n = (k - 1) * blocks + q
+            pl.loop(n * count // steps, (n + 1) * count // steps)(weigh)
+            for way in (1, -1):
+
+                @pl.when(has_behind(way, k))
+                def _():
+                    block = begun(way, k)
+                    line_copy(way, q, k - 1, block).wait_recv()
+                    if k < outer - 1:
+
+                        @pl.when(has_next(way))
+                        def _():
+                            line_copy(way, q, k, block).start()
+
+                    if inner == 2:
+                        d = k if way == 1 else outer - k
+                        near_do(q, d, lambda: near_copy(q, d, False).start())
+
+    if outer == 1:
+        pl.loop(0, count)(weigh)
+    for way in (1, -1):
+        last_but_one = row == (outer - 2 if way == 1 else 1)
+
+        if spare:
+
+            @pl.when(last_but_one)
+            def _():
+                for q in spare:
+                    near_copy(q, 0, True).wait_recv()
+                    extra_copy(way, q, row).start()
 
     lane = iota((brows, width), 1)
     slot_in = lane // (2 * total)
@@ -280,7 +370,19 @@
     for q in range(blocks):
         if inner == 2:
             for d in range(outer):
-                near_copy(q, d).wait_recv()
+                if not (d == 0 and q in spare):
+                    near_do(q, d, lambda: near_copy(q, d, True).wait_recv())
+        if q in spare:
+            @pl.when((row != 1) & (row != outer - 2))
+            def _():
+                near_copy(q, 0, True).wait_recv()
+
+            for way in (1, -1):
+
+                @pl.when(row == (outer - 1 if way == 1 else 0))
+                def _():
+                    extra_copy(way, q, begun(way, 1)).wait_recv()
+
         copy = pltpu.make_async_copy(spec.at[q], gathered.at[q], out_sem.at[q])
         copy.start()
         out_copies.append(copy)
@@ -317,13 +419,25 @@
         copy.start()
         beam_copies.append(copy)
     for q in range(blocks):
-        for d in range(1, outer):
-            far_copy(q, d).wait_send()
+        for way in (1, -1):
+            for k in range(outer - 1):
+
+                @pl.when(has_behind(way, k) & has_next(way))
+                def _():
+                    line_copy(way, q, k, begun(way, k)).wait_send()
+
+            if q in spare:
+
+                @pl.when(row == (outer - 2 if way == 1 else 1))
+                def _():
+                    extra_copy(way, q, row).wait_send()
+
         if inner == 2:
             for d in range(outer):
-                near_copy(q, d).wait_send()
-    for copy in turn_copies:
-        copy.wait_send()
+                near_do(q, d, lambda: near_copy(q, d, False).wait_send())
+    for q in range(parts):
+        for d in range(1, ng):
+            turn_copy(q, d).wait_send()
 
     @pl.when(grp < ng - 1)
     def _():
@@ -342,8 +456,9 @@
         copy.wait_send()
 
 
-def vis_kernel(here, total, per_tile, tiles, spec, vis):
+def vis_kernel(here, total, per_tile, tiles, spec, power, vis, series):
     width = spec.shape[2] // tiles
+    series[...] = power[...]
     mine = pl.ds(pl.multiple_of(lax.axis_index("sect") * here, 16), here)
     lane = iota((here, width), 1)
     slot_in = lane // (2 * total)
@@ -385,6 +500,8 @@
     outer = ns // 2 if ns % 2 == 0 else ns
     bf16, f32 = jnp.bfloat16, jnp.float32
     vmem = pl.BlockSpec(memory_space=pltpu.VMEM)
+    hbm = pl.BlockSpec(memory_space=pltpu.HBM)
+    parts = blocks if need % 128 == 0 else 1
     dims = (ns, ng, slots, here, th, inputs, beams)
     dma = pltpu.SemaphoreType.DMA
     gathered, series = pl.pallas_call(
@@ -393,9 +510,16 @@
             jax.ShapeDtypeStruct((blocks, inputs, BLOCK), bf16),
             jax.ShapeDtypeStruct((beams, th), f32),
         ),
-        in_specs=[vmem, vmem, vmem, pl.BlockSpec(memory_space=pltpu.SMEM), vmem, vmem, vmem],
+        in_specs=[hbm, hbm, hbm, pl.BlockSpec(memory_space=pltpu.SMEM), hbm, hbm, hbm],
         out_specs=(pl.BlockSpec(memory_space=pl.ANY), vmem),
         scratch_shapes=[
+            pltpu.VMEM(volts.shape, bf16),
+            pltpu.VMEM(pfb_window.shape, f32),
+            pltpu.VMEM((1, NCH), jnp.int32),
+            pltpu.VMEM(delays.shape, f32),
+            pltpu.VMEM((1, inputs), jnp.int32),
+            pltpu.VMEM((1, beams), jnp.int32),
+            dma((6,)),
             pltpu.VMEM((here, (TAPS - 1) * FRAME), bf16),
             pltpu.VMEM((FRAME, ng * lanes_g), bf16),
             pltpu.VMEM((th * lanes_g, chunk), bf16),
@@ -407,12 +531,14 @@
             pltpu.VMEM((blocks, inputs, BLOCK), bf16),
             pltpu.VMEM((ng + 1, brows, round_up(total, 128)), f32),
             dma((2,)),
-            dma((ng,)),
-            dma((ng,)),
+            dma((parts, ng)),
+            dma((parts, ng)),
+            dma((2, blocks, outer)),
+            dma((2, blocks, outer)),
             dma((blocks, outer)),
             dma((blocks, outer)),
-            dma((blocks, outer)),
-            dma((blocks, outer)),
+            dma((2, blocks)),
+            dma((2, blocks)),
             dma((ng,)),
             dma((ng,)),
             dma((blocks,)),
@@ -423,22 +549,33 @@
     )(
         volts,
         pfb_window,
-        chan_order.reshape(1, -1),
+        chan_order,
         chan_order,
         delays,
-        antenna_map.reshape(1, -1),
-        pointing.reshape(1, -1),
+        antenna_map,
+        pointing,
     )
-    vis = pl.pallas_call(
-        functools.partial(vis_kernel, here, total, per_tile, tiles),
-        grid=(blocks,),
-        out_shape=jax.ShapeDtypeStruct((slots, 2, here, inputs), f32),
-        in_specs=[pl.BlockSpec((1, inputs, BLOCK), lambda q: (q, 0, 0))],
-        out_specs=pl.BlockSpec(
-            (slots // blocks, 2, here, inputs), lambda q: (q, 0, 0, 0)
+    split = 2 if tiles % 2 == 0 else 1
+    small = pl.BlockSpec((beams, th), lambda q: (0, 0))
+    vis, series = pl.pallas_call(
+        functools.partial(vis_kernel, here, total, per_tile, tiles // split),
+        grid=(blocks * split,),
+        out_shape=(
+            jax.ShapeDtypeStruct((slots, 2, here, inputs), f32),
+            jax.ShapeDtypeStruct((beams, th), f32),
+        ),
+        in_specs=[
+            pl.BlockSpec((1, inputs, BLOCK // split), lambda q: (q // split, 0, q % split)),
+            small,
+        ],
+        out_specs=(
+            pl.BlockSpec(
+                (slots // (blocks * split), 2, here, inputs), lambda q: (q, 0, 0, 0)
+            ),
+            small,
         ),
         compiler_params=pltpu.CompilerParams(vmem_limit_bytes=48 * 1024 * 1024),
-    )(gathered)
+    )(gathered, series)
     return (vis, series)
 
 

time: 50.6 us -> 46 us (0.909)
  Pallas kernels: 44.5 us -> 39.9 us
    pallas_call x1, Pallas kernels: 39.9 us -> 33.8 us  [per_device(): pl.pallas_call(functools.partial(gather_kernel, dims), out_shape=(jax.Sha...]
    pallas_call x1, Pallas kernels: 4.62 us -> 6.02 us  [per_device(): pl.pallas_call(functools.partial(vis_kernel, here, total, per_tile, tiles...]
    reshape x1 -> x0, local copies, waits for them, and re-layouts: 0.68 us -> none  [per_device(): antenna_map.reshape(1, -1)]
    pallas_call x0 -> x1, local copies, waits for them, and re-layouts: none -> 0.65 us  [per_device(): pl.pallas_call(functools.partial(vis_kernel, here, total, per_tile, tiles...]
    unnamed x11 -> x12, local copies, waits for them, and re-layouts: 4.53 us -> 4.56 us
where the time goes in v2:
time: 46 us; the launch traced here: 45.7 us
  Pallas kernels  39.9 us (87%)
  local copies, waits for them, and re-layouts  5.21 us (11%)
  between operations  0.65 us (1%)
    pallas_call x1, Pallas kernels, per_device(): pl.pallas_call(functools.partial(gather_kernel, dims), out_shape=(jax.Sha...  33.8 us
    pallas_call x1, Pallas kernels, per_device(): pl.pallas_call(functools.partial(vis_kernel, here, total, per_tile, tiles...  6.02 us
    unnamed x12, local copies, waits for them, and re-layouts  4.56 us

profile of v2, /device:TPU:0, one launch (start us, length us, event | category | flops | bytes accessed | tf_op | source)
XLA Modules:
  0.0 45.7 jit_solution(7471369558375247914)
XLA Ops:
  0.6 0.0 copy-start
  0.6 0.9 %copy-done = bf16[48,2048]{1,0:T(8,128)(2,1)S(1)} copy-done((bf16[48,2048]{1,0:T(8,128)(2,1)S(1)}, bf16[48,2048]{1,0:T(8,128)(2,1)}, u32[]{:S(2)}) %copy-start) | copy-done | bytes 196632
  1.6 0.0 copy-start.1
  1.6 0.9 %copy-done.1 = f32[128,384]{1,0:T(8,128)S(1)} copy-done((f32[128,384]{1,0:T(8,128)S(1)}, f32[128,384]{1,0:T(8,128)}, u32[]{:S(2)}) %copy-start.1) | copy-done | bytes 196632
  2.5 0.0 copy-start.2
  2.5 0.7 %copy-done.2 = f32[4,512]{1,0:T(4,128)S(1)} copy-done((f32[4,512]{1,0:T(4,128)S(1)}, f32[4,512]{1,0:T(4,128)}, u32[]{:S(2)}) %copy-start.2) | copy-done | bytes 8216
  3.2 0.0 copy-start.3
  3.2 0.7 %copy-done.3 = s32[256]{0:T(256)S(1)} copy-done((s32[256]{0:T(256)S(1)}, s32[256]{0:T(256)}, u32[]{:S(2)}) %copy-start.3) | copy-done | bytes 1048
  3.9 0.0 copy-start.4
  3.9 0.7 %copy-done.4 = s32[384]{0:T(512)S(1)} copy-done((s32[384]{0:T(512)S(1)}, s32[384]{0:T(512)}, u32[]{:S(2)}) %copy-start.4) | copy-done | bytes 1560
  4.5 0.0 copy-start.5
  4.5 0.7 %copy-done.5 = s32[40]{0:T(128)S(1)} copy-done((s32[40]{0:T(128)S(1)}, s32[40]{0:T(128)}, u32[]{:S(2)}) %copy-start.5) | copy-done | bytes 184
  5.2 33.8 %shard_map.77 = (bf16[4,384,512]{2,1,0:T(8,128)(2,1)S(1)}, f32[40,4]{1,0:T(8,128)S(1)}) custom-call(bf16[48,2048]{1,0:T(8,128)(2,1)S(1)} %copy-done, f32[4,512]{1,0:T(4,128)S(1)} %copy-done.2, s32[256]{0:T(256)S(1)} %copy-done.3, s32[256]{0:T(256)S(1)} %copy-done.3, f32[128,384]{1,0:T(8,128)S(1)} %copy-done.1, s32[384]{0:T(512)S(1)} %copy-done.4, ...), custom_call_target="tpu_custom_call" | custom-call | tf_op jit(solution)/shard_map/pallas_call | solution.py:507
  39.0 6.0 %shard_map.78 = (f32[64,2,48,384]{3,2,1,0:T(8,128)}, f32[40,4]{1,0:T(8,128)S(1)}) custom-call(bf16[4,384,512]{2,1,0:T(8,128)(2,1)S(1)} %get-tuple-element.4.spec, f32[40,4]{1,0:T(8,128)S(1)} %get-tuple-element.5.power), custom_call_target="tpu_custom_call" | custom-call | tf_op jit(solution)/shard_map/pallas_call | solution.py:560
  45.1 0.7 %copy.8 = f32[40,4]{0,1:T(4,128)} copy(f32[40,4]{1,0:T(8,128)S(1)} %get-tuple-element.7) | data formatting | bytes 1280 | tf_op jit(solution)/shard_map/pallas_call | solution.py:560
Async XLA Ops:
  0.6 0.9 %copy-start = (bf16[48,2048]{1,0:T(8,128)(2,1)S(1)}, bf16[48,2048]{1,0:T(8,128)(2,1)}, u32[]{:S(2)}) copy-start(bf16[48,2048]{1,0:T(8,128)(2,1)} %volts_in.1) | copy-start | bytes 589828
  1.6 0.9 %copy-start.1 = (f32[128,384]{1,0:T(8,128)S(1)}, f32[128,384]{1,0:T(8,128)}, u32[]{:S(2)}) copy-start(f32[128,384]{1,0:T(8,128)} %delays_in.1) | copy-start | bytes 589828
  2.5 0.7 %copy-start.2 = (f32[4,512]{1,0:T(4,128)S(1)}, f32[4,512]{1,0:T(4,128)}, u32[]{:S(2)}) copy-start(f32[4,512]{1,0:T(4,128)} %pfb_in.1) | copy-start | bytes 24580
  3.2 0.7 %copy-start.3 = (s32[256]{0:T(256)S(1)}, s32[256]{0:T(256)}, u32[]{:S(2)}) copy-start(s32[256]{0:T(256)} %chan.1) | copy-start | bytes 3076
  3.9 0.7 %copy-start.4 = (s32[384]{0:T(512)S(1)}, s32[384]{0:T(512)}, u32[]{:S(2)}) copy-start(s32[384]{0:T(512)} %amap_in.1) | copy-start | bytes 4612
  4.5 0.7 %copy-start.5 = (s32[40]{0:T(128)S(1)}, s32[40]{0:T(128)}, u32[]{:S(2)}) copy-start(s32[40]{0:T(128)} %pointing_in.1) | copy-start | bytes 484

commit v3 on v2

--- a/solution.py
+++ b/solution.py
@@ -276,13 +276,29 @@
 
     spare = [q for q in range(blocks) if q >= blocks // 2] if inner == 2 and outer > 3 else []
 
+    def passes_on(way):
+        if way == 1:
+            return (row == 0) | (row == outer - 2)
+        return (row == 1) | (row == outer - 1)
+
+    def pass_on(at_end):
+        for way in (1, -1):
+            end = row == (0 if way == 1 else outer - 1)
+            last = row == (outer - 2 if way == 1 else 1)
+
+            @pl.when(end if at_end else last)
+            def _():
+                for q in spare:
+                    near_copy(q, 0, True).wait_recv()
+                    extra_copy(way, q, row).start()
+
     def by_line(q, d):
         if q not in spare:
             return None
         if d == outer - 1:
-            return row == 0
+            return passes_on(1)
         if d == 1:
-            return row == outer - 1
+            return passes_on(-1)
         return None
 
     def near_do(q, d, act):
@@ -348,18 +364,13 @@
                         d = k if way == 1 else outer - k
                         near_do(q, d, lambda: near_copy(q, d, False).start())
 
+        if k == 1 and spare:
+            pass_on(True)
+
     if outer == 1:
         pl.loop(0, count)(weigh)
-    for way in (1, -1):
-        last_but_one = row == (outer - 2 if way == 1 else 1)
-
-        if spare:
-
-            @pl.when(last_but_one)
-            def _():
-                for q in spare:
-                    near_copy(q, 0, True).wait_recv()
-                    extra_copy(way, q, row).start()
+    if spare:
+        pass_on(False)
 
     lane = iota((brows, width), 1)
     slot_in = lane // (2 * total)
@@ -373,13 +384,13 @@
                 if not (d == 0 and q in spare):
                     near_do(q, d, lambda: near_copy(q, d, True).wait_recv())
         if q in spare:
-            @pl.when((row != 1) & (row != outer - 2))
+            @pl.when(jnp.logical_not(passes_on(1) | passes_on(-1)))
             def _():
                 near_copy(q, 0, True).wait_recv()
 
             for way in (1, -1):
 
-                @pl.when(row == (outer - 1 if way == 1 else 0))
+                @pl.when(passes_on(-way))
                 def _():
                     extra_copy(way, q, begun(way, 1)).wait_recv()
 
@@ -428,7 +439,7 @@
 
             if q in spare:
 
-                @pl.when(row == (outer - 2 if way == 1 else 1))
+                @pl.when(passes_on(way))
                 def _():
                     extra_copy(way, q, row).wait_send()
 
@@ -451,14 +462,13 @@
         summed = summed + power[d + 1]
     lanes = summed.shape[1]
     turned = pltpu.roll(summed, lax.rem(lanes - grp * th, lanes), 1)
-    series[...] = turned[:beams, :th] * (1.0 / math.sqrt(NCH))
+    series[...] = turned.T[:th, :beams] * (1.0 / math.sqrt(NCH))
     for copy in beam_copies:
         copy.wait_send()
 
 
-def vis_kernel(here, total, per_tile, tiles, spec, power, vis, series):
+def vis_kernel(here, total, per_tile, tiles, spec, vis):
     width = spec.shape[2] // tiles
-    series[...] = power[...]
     mine = pl.ds(pl.multiple_of(lax.axis_index("sect") * here, 16), here)
     lane = iota((here, width), 1)
     slot_in = lane // (2 * total)
@@ -508,7 +518,7 @@
         functools.partial(gather_kernel, dims),
         out_shape=(
             jax.ShapeDtypeStruct((blocks, inputs, BLOCK), bf16),
-            jax.ShapeDtypeStruct((beams, th), f32),
+            jax.ShapeDtypeStruct((th, beams), f32),
         ),
         in_specs=[hbm, hbm, hbm, pl.BlockSpec(memory_space=pltpu.SMEM), hbm, hbm, hbm],
         out_specs=(pl.BlockSpec(memory_space=pl.ANY), vmem),
@@ -544,7 +554,7 @@
             dma((blocks,)),
         ],
         compiler_params=pltpu.CompilerParams(
-            collective_id=0, has_side_effects=True, vmem_limit_bytes=48 * 1024 * 1024
+            collective_id=0, has_side_effects=True, vmem_limit_bytes=63 * 1024 * 1024
         ),
     )(
         volts,
@@ -555,28 +565,17 @@
         antenna_map,
         pointing,
     )
-    split = 2 if tiles % 2 == 0 else 1
-    small = pl.BlockSpec((beams, th), lambda q: (0, 0))
-    vis, series = pl.pallas_call(
-        functools.partial(vis_kernel, here, total, per_tile, tiles // split),
-        grid=(blocks * split,),
-        out_shape=(
-            jax.ShapeDtypeStruct((slots, 2, here, inputs), f32),
-            jax.ShapeDtypeStruct((beams, th), f32),
+    vis = pl.pallas_call(
+        functools.partial(vis_kernel, here, total, per_tile, tiles),
+        grid=(blocks,),
+        out_shape=jax.ShapeDtypeStruct((slots, 2, here, inputs), f32),
+        in_specs=[pl.BlockSpec((1, inputs, BLOCK), lambda q: (q, 0, 0))],
+        out_specs=pl.BlockSpec(
+            (slots // blocks, 2, here, inputs), lambda q: (q, 0, 0, 0)
         ),
-        in_specs=[
-            pl.BlockSpec((1, inputs, BLOCK // split), lambda q: (q // split, 0, q % split)),
-            small,
-        ],
-        out_specs=(
-            pl.BlockSpec(
-                (slots // (blocks * split), 2, here, inputs), lambda q: (q, 0, 0, 0)
-            ),
-            small,
-        ),
-        compiler_params=pltpu.CompilerParams(vmem_limit_bytes=48 * 1024 * 1024),
-    )(gathered, series)
-    return (vis, series)
+        compiler_params=pltpu.CompilerParams(vmem_limit_bytes=63 * 1024 * 1024),
+    )(gathered)
+    return (vis, series.T)
 
 
 def solution(mesh):

time: 46 us -> 42 us (0.913)
  local copies, waits for them, and re-layouts: 5.21 us -> 0.58 us
  Pallas kernels: 39.9 us -> 40.6 us
    unnamed x12 -> x3, local copies, waits for them, and re-layouts: 4.56 us -> 0.58 us
    pallas_call x1 -> x0, local copies, waits for them, and re-layouts: 0.65 us -> none  [per_device(): pl.pallas_call(functools.partial(vis_kernel, here, total, per_tile, tiles...]
    pallas_call x1, Pallas kernels: 33.8 us -> 34.4 us  [per_device(): pl.pallas_call(functools.partial(gather_kernel, dims), out_shape=(jax.Sha...]
where the time goes in v3:
time: 42 us; the launch traced here: 41.8 us
  Pallas kernels  40.6 us (97%)
  between operations  0.65 us (2%)
  local copies, waits for them, and re-layouts  0.58 us (1%)
    pallas_call x1, Pallas kernels, per_device(): pl.pallas_call(functools.partial(gather_kernel, dims), out_shape=(jax.Sha...  34.4 us
    pallas_call x1, Pallas kernels, per_device(): pl.pallas_call(functools.partial(vis_kernel, here, total, per_tile, tiles...  6.13 us

profile of v3, /device:TPU:0, one launch (start us, length us, event | category | flops | bytes accessed | tf_op | source)
XLA Modules:
  0.0 41.8 jit_solution(13840186871738112752)
XLA Ops:
  0.6 34.4 %shard_map.77 = (bf16[4,384,512]{2,1,0:T(8,128)(2,1)}, f32[4,40]{1,0:T(4,128)}) custom-call(bf16[48,2048]{1,0:T(8,128)(2,1)} %volts_in.1, f32[4,512]{1,0:T(4,128)} %pfb_in.1, s32[256]{0:T(256)} %chan.1, s32[256]{0:T(256)} %chan.1, f32[128,384]{1,0:T(8,128)} %delays_in.1, s32[384]{0:T(512)} %amap_in.1, s32[40]{0:T(128)} %pointing_in.1), custom_call_target="tpu_custom_call" | custom-call | tf_op jit(solution)/shard_map/pallas_call | solution.py:517
  35.1 0.0 copy-start
  35.1 6.1 %shard_map.78 = f32[64,2,48,384]{3,2,1,0:T(8,128)} custom-call(bf16[4,384,512]{2,1,0:T(8,128)(2,1)} %get-tuple-element.4.spec), custom_call_target="tpu_custom_call" | custom-call | tf_op jit(solution)/shard_map/pallas_call | solution.py:568
  41.2 0.0 copy-done
  41.2 0.6 %copy.9 = f32[40,4]{0,1:T(4,128)} copy(f32[40,4]{0,1:T(4,128)S(1)} %bitcast.1) | data formatting | bytes 1280
Async XLA Ops:
  35.1 6.1 %copy-start = (f32[4,40]{1,0:T(4,128)S(1)}, f32[4,40]{1,0:T(4,128)}, u32[]{:S(2)}) copy-start(f32[4,40]{1,0:T(4,128)} %get-tuple-element.5) | copy-start | bytes 1924

commit v4 on v3

--- a/solution.py
+++ b/solution.py
@@ -573,7 +573,7 @@
         out_specs=pl.BlockSpec(
             (slots // blocks, 2, here, inputs), lambda q: (q, 0, 0, 0)
         ),
-        compiler_params=pltpu.CompilerParams(vmem_limit_bytes=63 * 1024 * 1024),
+        compiler_params=pltpu.CompilerParams(vmem_limit_bytes=48 * 1024 * 1024),
     )(gathered)
     return (vis, series.T)
 

time: 42 us -> 41.9 us (level)
  Pallas kernels: 40.6 us -> 39.1 us
  local copies, waits for them, and re-layouts: 0.58 us -> 1.98 us
    pallas_call x1, Pallas kernels: 6.13 us -> 4.62 us  [per_device(): pl.pallas_call(functools.partial(vis_kernel, here, total, per_tile, tiles...]
    unnamed x3 -> x5, local copies, waits for them, and re-layouts: 0.58 us -> 1.98 us
where the time goes in v4:
time: 41.9 us; the launch traced here: 41.7 us
  Pallas kernels  39.1 us (93%)
  local copies, waits for them, and re-layouts  1.98 us (5%)
  between operations  0.66 us (2%)
    pallas_call x1, Pallas kernels, per_device(): pl.pallas_call(functools.partial(gather_kernel, dims), out_shape=(jax.Sha...  34.5 us
    pallas_call x1, Pallas kernels, per_device(): pl.pallas_call(functools.partial(vis_kernel, here, total, per_tile, tiles...  4.62 us
    unnamed x5, local copies, waits for them, and re-layouts  1.98 us

profile of v4, /device:TPU:0, one launch (start us, length us, event | category | flops | bytes accessed | tf_op | source)
XLA Modules:
  0.0 41.7 jit_solution(9967623105016269900)
XLA Ops:
  0.6 34.5 %shard_map.77 = (bf16[4,384,512]{2,1,0:T(8,128)(2,1)}, f32[4,40]{1,0:T(4,128)}) custom-call(bf16[48,2048]{1,0:T(8,128)(2,1)} %volts_in.1, f32[4,512]{1,0:T(4,128)} %pfb_in.1, s32[256]{0:T(256)} %chan.1, s32[256]{0:T(256)} %chan.1, f32[128,384]{1,0:T(8,128)} %delays_in.1, s32[384]{0:T(512)} %amap_in.1, s32[40]{0:T(128)} %pointing_in.1), custom_call_target="tpu_custom_call" | custom-call | tf_op jit(solution)/shard_map/pallas_call | solution.py:517
  35.1 0.0 copy-start.1
  35.1 0.0 copy-start
  35.1 1.4 %copy-done = bf16[4,384,512]{2,1,0:T(8,128)(2,1)S(1)} copy-done((bf16[4,384,512]{2,1,0:T(8,128)(2,1)S(1)}, bf16[4,384,512]{2,1,0:T(8,128)(2,1)}, u32[]{:S(2)}) %copy-start) | copy-done | bytes 1572888
  36.5 4.6 %shard_map.78 = f32[64,2,48,384]{3,2,1,0:T(8,128)} custom-call(bf16[4,384,512]{2,1,0:T(8,128)(2,1)S(1)} %copy-done), custom_call_target="tpu_custom_call" | custom-call | tf_op jit(solution)/shard_map/pallas_call | solution.py:568
  41.1 0.0 copy-done.1
  41.1 0.6 %copy.9 = f32[40,4]{0,1:T(4,128)} copy(f32[40,4]{0,1:T(4,128)S(1)} %bitcast.1) | data formatting | bytes 1280
Async XLA Ops:
  35.1 6.0 %copy-start.1 = (f32[4,40]{1,0:T(4,128)S(1)}, f32[4,40]{1,0:T(4,128)}, u32[]{:S(2)}) copy-start(f32[4,40]{1,0:T(4,128)} %get-tuple-element.5) | copy-start | bytes 1924
  35.1 1.4 %copy-start = (bf16[4,384,512]{2,1,0:T(8,128)(2,1)S(1)}, bf16[4,384,512]{2,1,0:T(8,128)(2,1)}, u32[]{:S(2)}) copy-start(bf16[4,384,512]{2,1,0:T(8,128)(2,1)} %get-tuple-element.4.spec) | copy-start | bytes 4718596
